TPU v7x, 32 devices: a whole 2x2x4 slice. The times are simulated.
32 devices in a mesh: group: 2 (over y), dom: 4 (over z), dp: 2 (over x), feat: 2 (over core).
Axes of the slice: x: 2, y: 2, z: 4, core: 2. Of those that a mesh axis runs over, the one named last changes fastest.
Arguments:
- node_latents: bfloat16 [4, 384, 512], P(('group', 'dp'), 'dom', 'feat'), parts along dimension 0, may hold values from -6 to 6
- edge_latents: bfloat16 [4, 3072, 512], P(('group', 'dp'), 'dom', 'feat'), parts along dimension 0, may hold values from -6 to 6
- grad_nodes: bfloat16 [4, 384, 512], P(('group', 'dp'), 'dom', 'feat'), parts along dimension 0, may hold values from -6 to 6
- grad_edges: bfloat16 [4, 3072, 512], P(('group', 'dp'), 'dom', 'feat'), parts along dimension 0, may hold values from -6 to 6
- edge_sender: int32 [3072], P('dom'), may hold values from 0 to 143, as said below
- edge_receiver: int32 [3072], P('dom'), may hold values from -1 to 95, as said below
- halo_rows: int32 [4, 4, 12], P('dom'), may hold values from 0 to 95
- w_edge_in: bfloat16 [1536, 512], P(None, 'feat'), may hold values from -0.15625 to 0.15625
- w_edge_out: bfloat16 [512, 512], P(None, 'feat'), may hold values from -1 to 1
- w_node_in: bfloat16 [1024, 512], P(None, 'feat'), may hold values from -0.1875 to 0.1875
- w_node_out: bfloat16 [512, 512], P(None, 'feat'), may hold values from -1 to 1
Outputs:
- d_nodes: bfloat16 [4, 384, 512], P(('group', 'dp'), 'dom', 'feat'), parts along dimension 0
- d_edges: bfloat16 [4, 3072, 512], P(('group', 'dp'), 'dom', 'feat'), parts along dimension 0
- dw_edge_in: float32 [3072, 512], P(('group', 'dp'), 'feat'), parts along dimension 0
- dw_edge_out: float32 [1024, 512], P(('group', 'dp'), 'feat'), parts along dimension 0
- dw_node_in: float32 [2048, 512], P(('group', 'dp'), 'feat'), parts along dimension 0
- dw_node_out: float32 [1024, 512], P(('group', 'dp'), 'feat'), parts along dimension 0
There are 2 independent parts, one for each index of `group`. A program takes and returns all parts, laid end to end along the dimension named above; an argument that names none is the same for every part. Nothing has to cross between parts.
Inputs may be any that keep to these rules, and one draw needn't show every extreme that they name: `edge_receiver`: in each partition's 768 slots the live edges come first and each holds a receiver of that partition; every later slot holds -1. Each partition has at least max(96, 4) live slots, and in every draw some partition has all 768 live. `edge_sender`: A value t below 96 names node t of the slot's own partition; t = 96 + q * 12 + k names what partition q sends to the slot's partition in halo slot k, with q never the slot's own partition. Padding slots hold 0.
All inputs are finite; a program needn't handle non-finite values.
Results may differ from a plain program's by a relative error of at most 0.014.
Values may be sent and summed in bfloat16 or wider, within the bound.
A program may use at most 64 MiB of HBM per device.

v0:
```python
import math

import jax
import jax.numpy as jnp
from jax import lax
from jax.sharding import PartitionSpec as P

EPSILON = 1e-05


def silu_slope(preact):
    sigmoid = jax.nn.sigmoid(preact)
    return sigmoid * (1.0 + preact * (1.0 - sigmoid))


def product(first, second):
    return jnp.dot(first, second, preferred_element_type=jnp.float32)


def product_tn(first, second):
    return lax.dot_general(
        first, second, (((0,), (0,)), ((), ())), preferred_element_type=jnp.float32
    )


def product_nt(first, second):
    return lax.dot_general(
        first, second, (((1,), (1,)), ((), ())), preferred_element_type=jnp.float32
    )


def widen_one(pieces):
    return lax.all_gather(pieces, "feat", axis=1, tiled=True)


def widen_pair(first, second):
    return (
        lax.all_gather(first, "feat", axis=1, tiled=True),
        lax.all_gather(second, "feat", axis=1, tiled=True),
    )


def feat_total(values):
    return lax.psum(values, "feat")


def feat_pair(first, second):
    return lax.psum((first, second), "feat")


def norm_forward(values, full_width):
    row_mean = feat_total(jnp.sum(values, axis=1, keepdims=True)) / full_width
    centered = values - row_mean
    spread = feat_total(jnp.sum(centered * centered, axis=1, keepdims=True)) / full_width
    inverse = lax.rsqrt(spread + EPSILON)
    return (centered * inverse, inverse)


def norm_backward(upstream, normed, inverse, full_width):
    grad_sum, cross_sum = feat_pair(
        jnp.sum(upstream, axis=1, keepdims=True), jnp.sum(upstream * normed, axis=1, keepdims=True)
    )
    return inverse * (upstream - grad_sum / full_width - normed * (cross_sum / full_width))


def own_rows(weights, groups, model_width, half_width, feat_index):
    shaped = weights.reshape(groups, model_width, weights.shape[1])
    picked = lax.dynamic_slice_in_dim(shaped, feat_index * half_width, half_width, 1)
    return picked.reshape(groups * half_width, weights.shape[1])


def shards(
    node_latents,
    edge_latents,
    grad_nodes,
    grad_edges,
    edge_sender,
    edge_receiver,
    halo_rows,
    w_edge_in,
    w_edge_out,
    w_node_in,
    w_node_out,
):
    nodes_here = node_latents[0]
    edges_here = edge_latents[0]
    upstream_nodes = grad_nodes[0].astype(jnp.float32)
    upstream_edges = grad_edges[0].astype(jnp.float32)
    node_count = nodes_here.shape[0]
    edge_count = edges_here.shape[0]
    half_width = nodes_here.shape[1]
    model_width = half_width * lax.axis_size("feat")
    feat_index = lax.axis_index("feat")
    hidden_half = w_edge_in.shape[1]
    full_in, full_out, node_in_full, node_out_full = (
        lax.all_gather(w_edge_in, "feat", axis=1, tiled=True),
        lax.all_gather(w_edge_out, "feat", axis=1, tiled=True),
        lax.all_gather(w_node_in, "feat", axis=1, tiled=True),
        lax.all_gather(w_node_out, "feat", axis=1, tiled=True),
    )
    send_rows = halo_rows[0]
    outgoing = jnp.take(nodes_here, send_rows.reshape(-1), axis=0).reshape(
        send_rows.shape + (half_width,)
    )
    incoming = lax.all_to_all(outgoing, "dom", split_axis=0, concat_axis=0, tiled=True)
    node_table = jnp.concatenate([nodes_here, incoming.reshape(-1, half_width)], axis=0)
    edges_full, table_full = widen_pair(edges_here, node_table)
    live_rows = (edge_receiver >= 0)[:, None]
    table_index = jnp.arange(node_table.shape[0], dtype=jnp.int32)
    node_index = jnp.arange(node_count, dtype=jnp.int32)
    sender_hot = (edge_sender[:, None] == table_index[None, :]).astype(jnp.bfloat16)
    receiver_hot = (edge_receiver[:, None] == node_index[None, :]).astype(jnp.bfloat16)
    send_latents = product(sender_hot, table_full).astype(jnp.bfloat16)
    recv_latents = product(receiver_hot, table_full[:node_count]).astype(jnp.bfloat16)
    edge_input = jnp.concatenate([edges_full, send_latents, recv_latents], axis=1)
    edge_pre = product(edge_input, w_edge_in)
    edge_act = jax.nn.silu(edge_pre).astype(jnp.bfloat16)
    edge_act_full = widen_one(edge_act)
    edge_normed, edge_inverse = norm_forward(product(edge_act_full, w_edge_out), model_width)
    message = jnp.where(live_rows, edge_normed, 0.0).astype(jnp.bfloat16)
    summed = product_tn(receiver_hot, message).astype(jnp.bfloat16)
    nodes_full, summed_full = widen_pair(nodes_here, summed)
    node_input = jnp.concatenate([nodes_full, summed_full], axis=1)
    node_pre = product(node_input, w_node_in)
    node_act = jax.nn.silu(node_pre).astype(jnp.bfloat16)
    node_act_full = widen_one(node_act)
    node_normed, node_inverse = norm_forward(product(node_act_full, w_node_out), model_width)
    node_out_grad = norm_backward(upstream_nodes, node_normed, node_inverse, model_width).astype(
        jnp.bfloat16
    )
    dw_node_out = product_tn(node_act_full, node_out_grad)
    node_out_grad_full = widen_one(node_out_grad)
    node_hidden_rows = lax.dynamic_slice_in_dim(
        node_out_full, feat_index * hidden_half, hidden_half, 0
    )
    node_pre_grad = (
        product_nt(node_out_grad_full, node_hidden_rows) * silu_slope(node_pre)
    ).astype(jnp.bfloat16)
    dw_node_in = product_tn(node_input, node_pre_grad)
    node_pre_grad_full = widen_one(node_pre_grad)
    node_input_grad = product_nt(
        node_pre_grad_full, own_rows(node_in_full, 2, model_width, half_width, feat_index)
    )
    direct_grad = node_input_grad[:, :half_width]
    summed_grad = node_input_grad[:, half_width:].astype(jnp.bfloat16)
    message_grad = jnp.where(live_rows, upstream_edges + product(receiver_hot, summed_grad), 0.0)
    edge_out_grad = norm_backward(message_grad, edge_normed, edge_inverse, model_width).astype(
        jnp.bfloat16
    )
    dw_edge_out = product_tn(edge_act_full, edge_out_grad)
    edge_out_grad_full = widen_one(edge_out_grad)
    edge_hidden_rows = lax.dynamic_slice_in_dim(full_out, feat_index * hidden_half, hidden_half, 0)
    edge_pre_grad = (
        product_nt(edge_out_grad_full, edge_hidden_rows) * silu_slope(edge_pre)
    ).astype(jnp.bfloat16)
    dw_edge_in = product_tn(edge_input, edge_pre_grad)
    edge_pre_grad_full = widen_one(edge_pre_grad)
    edge_input_grad = product_nt(
        edge_pre_grad_full, own_rows(full_in, 3, model_width, half_width, feat_index)
    ).astype(jnp.bfloat16)
    edge_result = (upstream_edges + edge_input_grad[:, :half_width].astype(jnp.float32)).astype(
        jnp.bfloat16
    )
    table_grad = product_tn(sender_hot, edge_input_grad[:, half_width : 2 * half_width])
    returned = lax.all_to_all(
        table_grad[node_count:].reshape(incoming.shape).astype(jnp.bfloat16),
        "dom",
        split_axis=0,
        concat_axis=0,
        tiled=True,
    ).astype(jnp.float32)
    send_hot = (send_rows.reshape(-1)[None, :] == node_index[:, None]).astype(jnp.float32)
    back_sum = jnp.dot(
        send_hot,
        returned.reshape(-1, half_width),
        precision=lax.Precision.HIGHEST,
        preferred_element_type=jnp.float32,
    )
    node_grad = (
        direct_grad
        + product_tn(receiver_hot, edge_input_grad[:, 2 * half_width :])
        + table_grad[:node_count]
        + back_sum
    )
    node_result = node_grad.astype(jnp.bfloat16)
    edge_factor = 1.0 / math.sqrt(lax.axis_size("dp") * edge_count * lax.axis_size("dom"))
    node_factor = 1.0 / math.sqrt(lax.axis_size("dp") * node_count * lax.axis_size("dom"))
    grad_edge_in = dw_edge_in * edge_factor
    grad_edge_out = dw_edge_out * edge_factor
    grad_node_in = dw_node_in * node_factor
    grad_node_out = dw_node_out * node_factor
    shares = (
        lax.psum_scatter(
            grad_edge_in.astype(jnp.bfloat16), "dp", scatter_dimension=0, tiled=True
        ).astype(jnp.float32),
        lax.psum_scatter(
            grad_edge_out.astype(jnp.bfloat16), "dp", scatter_dimension=0, tiled=True
        ).astype(jnp.float32),
        lax.psum_scatter(
            grad_node_in.astype(jnp.bfloat16), "dp", scatter_dimension=0, tiled=True
        ).astype(jnp.float32),
        lax.psum_scatter(
            grad_node_out.astype(jnp.bfloat16), "dp", scatter_dimension=0, tiled=True
        ).astype(jnp.float32),
    )
    weight_grads = (
        lax.psum(shares[0].astype(jnp.bfloat16), "dom").astype(jnp.float32),
        lax.psum(shares[1].astype(jnp.bfloat16), "dom").astype(jnp.float32),
        lax.psum(shares[2].astype(jnp.bfloat16), "dom").astype(jnp.float32),
        lax.psum(shares[3].astype(jnp.bfloat16), "dom").astype(jnp.float32),
    )
    return (
        node_result[None],
        edge_result[None],
        weight_grads[0],
        weight_grads[1],
        weight_grads[2],
        weight_grads[3],
    )


def solution(mesh):
    return jax.shard_map(
        shards,
        mesh=mesh,
        in_specs=(
            P(("group", "dp"), "dom", "feat"),
            P(("group", "dp"), "dom", "feat"),
            P(("group", "dp"), "dom", "feat"),
            P(("group", "dp"), "dom", "feat"),
            P("dom"),
            P("dom"),
            P("dom", None, None),
            P(None, "feat"),
            P(None, "feat"),
            P(None, "feat"),
            P(None, "feat"),
        ),
        out_specs=(
            P(("group", "dp"), "dom", "feat"),
            P(("group", "dp"), "dom", "feat"),
            P(("group", "dp"), "feat"),
            P(("group", "dp"), "feat"),
            P(("group", "dp"), "feat"),
            P(("group", "dp"), "feat"),
        ),
        check_vma=False,
    )
```

profile of v0, /device:TPU:0, one launch (start us, length us, event | category | flops | bytes accessed | tf_op | source)
XLA Modules:
  0.0 181.4 jit_solution(5986286570927042965)
XLA Ops:
  8.1 0.7 all-gather.5.cloned.1.call-update
  8.7 0.8 reshape_squeeze.8
  9.5 1.5 gather_fusion
  11.0 0.7 compare_and_fusion
  11.7 0.7 broadcast_select_fusion
  12.4 6.3 %all-to-all-start = ((bf16[4,12,256]{2,1,0:T(8,128)(2,1)}), bf16[4,12,256]{2,1,0:T(8,128)(2,1)S(1)}, u32[]{:S(2)}, u32[]{:S(2)}) async-start(bf16[4,12,256]{2,1,0:T(8,128)(2,1)} %broadcast_select_fusion), calls=%async_computation | async-start | bytes 65536 | tf_op jit(solution)/shard_map/all_to_all | solution.py:105
  18.8 0.7 all-gather.7.cloned.1.call-update
  19.6 0.2 copy.21
  19.8 2.8 %all-gather.1 = bf16[1,768,512]{1,2,0:T(8,128)(2,1)S(1)} all-gather(bf16[1,768,256]{1,2,0:T(8,128)(2,1)S(1)} %copy.21), channel_id=3, replica_groups=mesh['group'=2,'dom'=4,'dp'=2,'feat'=2] {'feat'}, dimensions={2}, use_global_device_ids=true | all-gather | bytes 1179648 | tf_op jit(solution)/shard_map/all_gather | solution.py:38
  22.6 2.4 %all_gather.49 = bf16[512,512]{1,0:T(8,128)(2,1)} all-gather(bf16[512,256]{1,0:T(8,128)(2,1)S(1)} %copy-done.2), channel_id=1, replica_groups=mesh['group'=2,'dom'=4,'dp'=2,'feat'=2] {'feat'}, dimensions={1}, use_global_device_ids=true | all-gather | bytes 786432 | tf_op jit(solution)/shard_map/all_gather | solution.py:99
  25.2 1.9 %all-gather = bf16[1,96,512]{2,1,0:T(8,128)(2,1)S(1)} all-gather(bf16[1,96,256]{2,1,0:T(8,128)(2,1)S(1)} %copy-done), channel_id=2, replica_groups=mesh['group'=2,'dom'=4,'dp'=2,'feat'=2] {'feat'}, dimensions={2}, use_global_device_ids=true | all-gather | bytes 147456 | tf_op jit(solution)/shard_map/all_gather | solution.py:38
  27.1 1.9 %all_gather.44 = bf16[144,512]{1,0:T(8,128)(2,1)S(1)} all-gather(bf16[144,256]{1,0:T(8,128)(2,1)S(1)} %pad_maximum_fusion.6), channel_id=1, replica_groups=mesh['group'=2,'dom'=4,'dp'=2,'feat'=2] {'feat'}, dimensions={1}, use_global_device_ids=true | all-gather | bytes 221184 | tf_op jit(solution)/shard_map/all_gather | solution.py:39
  29.0 0.5 convolution_convert_fusion.1
  29.5 0.6 convolution_convert_fusion.2
  30.1 1.7 multiply_convert_fusion.1
  31.8 2.8 %all_gather.45 = bf16[768,512]{1,0:T(8,128)(2,1)S(1)} all-gather(bf16[768,256]{1,0:T(8,128)(2,1)S(1)} %get-tuple-element.28), channel_id=1, replica_groups=mesh['group'=2,'dom'=4,'dp'=2,'feat'=2] {'feat'}, dimensions={1}, use_global_device_ids=true | all-gather | bytes 1179648 | tf_op jit(solution)/shard_map/all_gather | solution.py:33
  34.7 0.4 fusion.51
  35.1 2.5 %psum.84 = f32[768,1]{0,1:T(1,128)S(1)} all-reduce(f32[768,1]{0,1:T(1,128)S(1)} %broadcast_in_dim.65), channel_id=1, replica_groups=mesh['group'=2,'dom'=4,'dp'=2,'feat'=2] {'feat'}, use_global_device_ids=true, to_apply=%region_1.2 | all-reduce | flops 768 | bytes 6144 | tf_op jit(solution)/shard_map/psum | solution.py:44
  37.8 2.5 %psum.85 = f32[768,1]{0,1:T(1,128)S(1)} all-reduce(f32[768,1]{0,1:T(1,128)S(1)} %broadcast_in_dim.66), channel_id=1, replica_groups=mesh['group'=2,'dom'=4,'dp'=2,'feat'=2] {'feat'}, use_global_device_ids=true, to_apply=%region_3.4 | all-reduce | flops 768 | bytes 6144 | tf_op jit(solution)/shard_map/psum | solution.py:44
  40.3 0.4 convolution_convert_fusion.3
  40.7 1.9 %all_gather.46 = bf16[96,512]{1,0:T(8,128)(2,1)S(1)} all-gather(bf16[96,256]{1,0:T(8,128)(2,1)S(1)} %convolution_convert_fusion.3), channel_id=1, replica_groups=mesh['group'=2,'dom'=4,'dp'=2,'feat'=2] {'feat'}, dimensions={1}, use_global_device_ids=true | all-gather | bytes 147456 | tf_op jit(solution)/shard_map/all_gather | solution.py:39
  42.6 0.9 multiply_convert_fusion.2
  43.5 1.9 %all_gather.47 = bf16[96,512]{1,0:T(8,128)(2,1)S(1)} all-gather(bf16[96,256]{1,0:T(8,128)(2,1)S(1)} %get-tuple-element.32), channel_id=1, replica_groups=mesh['group'=2,'dom'=4,'dp'=2,'feat'=2] {'feat'}, dimensions={1}, use_global_device_ids=true | all-gather | bytes 147456 | tf_op jit(solution)/shard_map/all_gather | solution.py:33
  45.3 0.3 fusion.52
  45.6 2.5 %psum.86 = f32[96,1]{0,1:T(1,128)S(1)} all-reduce(f32[96,1]{0,1:T(1,128)S(1)} %bitcast.80), channel_id=1, replica_groups=mesh['group'=2,'dom'=4,'dp'=2,'feat'=2] {'feat'}, use_global_device_ids=true, to_apply=%region_5.6 | all-reduce | flops 96 | bytes 768 | tf_op jit(solution)/shard_map/psum | solution.py:44
  48.1 0.2 multiply_reduce_fusion.2
  48.3 2.5 %psum.87 = f32[96,1]{0,1:T(1,128)S(1)} all-reduce(f32[96,1]{0,1:T(1,128)S(1)} %bitcast.79), channel_id=1, replica_groups=mesh['group'=2,'dom'=4,'dp'=2,'feat'=2] {'feat'}, use_global_device_ids=true, to_apply=%region_7.8 | all-reduce | flops 96 | bytes 768 | tf_op jit(solution)/shard_map/psum | solution.py:44
  50.8 0.2 fusion.39
  50.9 2.5 %all-reduce.1 = (f32[96,1]{0,1:T(1,128)S(1)}, f32[96,1]{0,1:T(1,128)S(1)}) all-reduce(f32[96,1]{0,1:T(1,128)S(1)} %bitcast.78, f32[96,1]{0,1:T(1,128)S(1)} %bitcast.77), channel_id=1, replica_groups=mesh['group'=2,'dom'=4,'dp'=2,'feat'=2] {'feat'}, use_global_device_ids=true, to_apply=%region_11.12 | all-reduce | flops 192 | bytes 1536 | tf_op jit(solution)/shard_map/psum | solution.py:48
  53.5 1.0 fusion.4
  54.6 2.2 %all_gather.53 = bf16[512,512]{1,0:T(8,128)(2,1)S(1)} all-gather(bf16[512,256]{1,0:T(8,128)(2,1)S(1)} %copy-done.1), channel_id=1, replica_groups=mesh['group'=2,'dom'=4,'dp'=2,'feat'=2] {'feat'}, dimensions={1}, use_global_device_ids=true | all-gather | bytes 786432 | tf_op jit(solution)/shard_map/all_gather | solution.py:97
  56.8 0.2 copy.22
  56.9 1.9 %all_gather.48 = bf16[96,512]{1,0:T(8,128)(2,1)S(1)} all-gather(bf16[96,256]{1,0:T(8,128)(2,1)S(1)} %fusion.38), channel_id=1, replica_groups=mesh['group'=2,'dom'=4,'dp'=2,'feat'=2] {'feat'}, dimensions={1}, use_global_device_ids=true | all-gather | bytes 147456 | tf_op jit(solution)/shard_map/all_gather | solution.py:33
  58.8 1.1 fusion.8
  59.9 1.9 %all_gather.50 = bf16[96,512]{1,0:T(8,128)(2,1)S(1)} all-gather(bf16[96,256]{1,0:T(8,128)(2,1)S(1)} %fusion.8), channel_id=1, replica_groups=mesh['group'=2,'dom'=4,'dp'=2,'feat'=2] {'feat'}, dimensions={1}, use_global_device_ids=true | all-gather | bytes 147456 | tf_op jit(solution)/shard_map/all_gather | solution.py:33
  61.8 2.0 %fusion.1 = bf16[1024,256]{1,0:T(8,128)(2,1)} fusion(bf16[96,256]{1,0:T(8,128)(2,1)S(1)} %fusion.8, bf16[96,512]{1,0:T(8,128)(2,1)} %copy-done.20, bf16[96,512]{1,0:T(8,128)(2,1)S(1)} %bitcast.76), kind=kOutput, calls=%fused_computation.8 | convolution fusion | flops 51249152 | bytes 770048 | tf_op jit(solution)/shard_map/dot_general | solution.py:21
  64.0 1.1 constant_dynamic-slice_fusion.1
  65.1 0.3 fusion.53
  65.4 0.7 copy-done.14
  66.0 0.5 fusion.50
  66.6 2.5 %all-reduce = (f32[768,1]{0,1:T(1,128)S(1)}, f32[768,1]{0,1:T(1,128)S(1)}) all-reduce(f32[768,1]{0,1:T(1,128)S(1)} %broadcast_in_dim.73, f32[768,1]{0,1:T(1,128)S(1)} %broadcast_in_dim.72), channel_id=1, replica_groups=mesh['group'=2,'dom'=4,'dp'=2,'feat'=2] {'feat'}, use_global_device_ids=true, to_apply=%region_15.16 | all-reduce | flops 1536 | bytes 12288 | tf_op jit(solution)/shard_map/psum | solution.py:48
  69.1 0.2 multiply_convert_fusion
  69.3 2.4 %all_gather.52 = bf16[768,512]{0,1:T(8,128)(2,1)S(1)} all-gather(bf16[768,256]{0,1:T(8,128)(2,1)S(1)} %multiply_convert_fusion), channel_id=1, replica_groups=mesh['group'=2,'dom'=4,'dp'=2,'feat'=2] {'feat'}, dimensions={1}, use_global_device_ids=true | all-gather | bytes 1179648 | tf_op jit(solution)/shard_map/all_gather | solution.py:33
  71.7 1.1 fusion.5
  72.9 1.8 fusion.3
  74.7 1.7 fusion
  76.6 2.4 %all_gather.54 = bf16[768,512]{1,0:T(8,128)(2,1)S(1)} all-gather(bf16[768,256]{1,0:T(8,128)(2,1)S(1)} %fusion.3), channel_id=1, replica_groups=mesh['group'=2,'dom'=4,'dp'=2,'feat'=2] {'feat'}, dimensions={1}, use_global_device_ids=true | all-gather | bytes 1179648 | tf_op jit(solution)/shard_map/all_gather | solution.py:33
  78.9 1.2 constant_dynamic-slice_fusion
  80.2 4.5 %reduce-scatter.9.cloned.1.call-done = bf16[512,256]{1,0:T(8,128)(2,1)} async-done(((bf16[1024,256]{1,0:T(8,128)(2,1)}), bf16[512,256]{1,0:T(8,128)(2,1)}) %reduce-scatter.9.cloned.1.call-update) | async-done | bytes 262160 | tf_op jit(solution)/shard_map/reduce_scatter | solution.py:199
  84.6 14.3 %reduce-scatter.7.cloned.1.call-done = bf16[256,256]{1,0:T(8,128)(2,1)} async-done(((bf16[512,256]{1,0:T(8,128)(2,1)}), bf16[256,256]{1,0:T(8,128)(2,1)}) %reduce-scatter.7.cloned.1.call-update) | async-done | bytes 131088 | tf_op jit(solution)/shard_map/reduce_scatter | solution.py:196
  98.9 20.3 %reduce-scatter.5.cloned.1.call-done = bf16[768,256]{1,0:T(8,128)(2,1)} async-done(((bf16[1536,256]{1,0:T(8,128)(2,1)}), bf16[768,256]{1,0:T(8,128)(2,1)}) %reduce-scatter.5.cloned.1.call-update) | async-done | bytes 393232 | tf_op jit(solution)/shard_map/reduce_scatter | solution.py:193
  119.3 0.8 convolution_convert_fusion
  120.1 0.4 fusion.13
  120.5 0.6 convert_element_type.110
  121.2 4.6 %all-to-all-start.1 = ((bf16[4,12,256]{2,1,0:T(8,128)(2,1)}), bf16[4,12,256]{2,1,0:T(8,128)(2,1)S(1)}, u32[]{:S(2)}, u32[]{:S(2)}) async-start(bf16[4,12,256]{2,1,0:T(8,128)(2,1)} %convert_element_type.110), calls=%async_computation.1 | async-start | bytes 65536 | tf_op jit(solution)/shard_map/all_to_all | solution.py:165
  125.9 0.4 fusion.6
  126.3 0.9 copy.24
  127.2 4.3 %all-to-all-done.1 = bf16[4,12,256]{2,1,0:T(8,128)(2,1)S(1)} async-done(((bf16[4,12,256]{2,1,0:T(8,128)(2,1)}), bf16[4,12,256]{2,1,0:T(8,128)(2,1)S(1)}, u32[]{:S(2)}, u32[]{:S(2)}) %all-to-all-start.1) | async-done | bytes 24608 | tf_op jit(solution)/shard_map/all_to_all | solution.py:165
  131.6 0.8 fusion.9
  132.3 36.5 %all-reduce.5.cloned.1.call-done = (bf16[768,256]{1,0:T(8,128)(2,1)}, bf16[256,256]{1,0:T(8,128)(2,1)}, bf16[512,256]{1,0:T(8,128)(2,1)}, bf16[256,256]{1,0:T(8,128)(2,1)}) async-done(((bf16[768,256]{1,0:T(8,128)(2,1)}, bf16[256,256]{1,0:T(8,128)(2,1)}, bf16[512,256]{1,0:T(8,128)(2,1)}, bf16[256,256]{1,0:T(8,128)(2,1)}), (bf16[768,256]{1,0:T(8,128)(2,1)}, bf16[256,256]{1,0:T(8,128)(2,1)}, ...) | async-done | bytes 917520 | tf_op jit(solution)/shard_map/psum | solution.py:207
  168.8 2.0 %convert_element_type.115 = f32[768,256]{1,0:T(8,128)} convert(bf16[768,256]{1,0:T(8,128)(2,1)} %get-tuple-element.24) | non-fusion elementwise | flops 196608 | bytes 1179648 | tf_op jit(solution)/shard_map/convert_element_type | solution.py:207
  170.8 1.8 convert_element_type.119
  172.6 0.7 convert_element_type.117
  173.3 0.7 convert_element_type.121
  (103 shorter events, 1.2 us)
Async XLA Ops:
  8.0 11.6 %copy-start.16 = (bf16[1,768,256]{2,1,0:T(8,128)(2,1)S(1)}, bf16[1,768,256]{2,1,0:T(8,128)(2,1)}, u32[]{:S(2)}) copy-start(bf16[1,768,256]{2,1,0:T(8,128)(2,1)} %param.12) | copy-start | bytes 1179652
  8.0 56.0 %all-gather.5.cloned.1.call-start = ((), (), s32[]{:S(2)}) async-start(), calls=%async_computation.6 | async-start | bytes 1572864 | tf_op jit(solution)/shard_map/all_gather | solution.py:98
  9.5 13.0 %copy-start.23 = (s32[768]{0:T(1024)S(1)}, s32[768]{0:T(1024)}, u32[]{:S(2)}) copy-start(s32[768]{0:T(1024)} %param.16) | copy-start | bytes 9220
  9.5 13.0 %copy-start.2 = (bf16[512,256]{1,0:T(8,128)(2,1)S(1)}, bf16[512,256]{1,0:T(8,128)(2,1)}, u32[]{:S(2)}) copy-start(bf16[512,256]{1,0:T(8,128)(2,1)} %param.21) | copy-start | bytes 786436
  12.4 14.6 %all-to-all-start = ((bf16[4,12,256]{2,1,0:T(8,128)(2,1)}), bf16[4,12,256]{2,1,0:T(8,128)(2,1)S(1)}, u32[]{:S(2)}, u32[]{:S(2)}) async-start(bf16[4,12,256]{2,1,0:T(8,128)(2,1)} %broadcast_select_fusion), calls=%async_computation | async-start | bytes 65536 | tf_op jit(solution)/shard_map/all_to_all | solution.py:105
  18.7 60.2 %all-gather.7.cloned.1.call-start = ((), (), s32[]{:S(2)}) async-start(), calls=%async_computation.7 | async-start | bytes 2359296 | tf_op jit(solution)/shard_map/all_gather | solution.py:96
  19.5 5.6 %copy-start.12 = (bf16[1,96,256]{2,1,0:T(8,128)(2,1)S(1)}, bf16[1,96,256]{2,1,0:T(8,128)(2,1)}, u32[]{:S(2)}) copy-start(bf16[1,96,256]{2,1,0:T(8,128)(2,1)} %param.13) | copy-start | bytes 147460
  19.5 5.7 %copy-start = (bf16[1,96,256]{2,1,0:T(8,128)(2,1)S(1)}, bf16[1,96,256]{2,1,0:T(8,128)(2,1)}, u32[]{:S(2)}) copy-start(bf16[1,96,256]{2,1,0:T(8,128)(2,1)} %param.11) | copy-start | bytes 147460
  19.5 60.6 %reduce-scatter.11.cloned.1.call-start = ((), (), s32[]{:S(2)}) async-start(), calls=%async_computation.11 | async-start | bytes 393216 | tf_op jit(solution)/shard_map/reduce_scatter | solution.py:202
  19.7 9.8 %copy-start.28 = (s32[768]{0:T(1024)S(1)}, s32[768]{0:T(1024)}, u32[]{:S(2)}) copy-start(s32[768]{0:T(1024)} %param.15) | copy-start | bytes 9220
  22.5 7.6 %copy-start.4 = (bf16[1,768,512]{1,2,0:T(8,128)(2,1)}, bf16[1,768,512]{1,2,0:T(8,128)(2,1)S(1)}, u32[]{:S(2)}) copy-start(bf16[1,768,512]{1,2,0:T(8,128)(2,1)S(1)} %all-gather.1) | copy-start | bytes 2359300
  22.6 17.7 %copy-start.30 = (pred[768]{0:T(1024)(128)(4,1)}, pred[768]{0:T(1024)(128)(4,1)S(1)}, u32[]{:S(2)}) copy-start(pred[768]{0:T(1024)(128)(4,1)S(1)} %broadcast_compare_fusion) | copy-start | bytes 2308
  22.6 7.5 %copy-start.3 = (bf16[1536,256]{1,0:T(8,128)(2,1)S(1)}, bf16[1536,256]{1,0:T(8,128)(2,1)}, u32[]{:S(2)}) copy-start(bf16[1536,256]{1,0:T(8,128)(2,1)} %param.18) | copy-start | bytes 2359300
  29.5 2.3 %copy-start.6 = (bf16[768,512]{0,1:T(8,128)(2,1)}, bf16[768,512]{0,1:T(8,128)(2,1)S(1)}, u32[]{:S(2)}) copy-start(bf16[768,512]{0,1:T(8,128)(2,1)S(1)} %convolution_convert_fusion.1) | copy-start | bytes 2359300
  30.1 1.8 copy-start.8
  30.1 4.6 %copy-start.1 = (bf16[512,256]{1,0:T(8,128)(2,1)S(1)}, bf16[512,256]{1,0:T(8,128)(2,1)}, u32[]{:S(2)}) copy-start(bf16[512,256]{1,0:T(8,128)(2,1)} %param.19) | copy-start | bytes 786436
  34.7 7.9 %copy-start.11 = (bf16[1024,256]{1,0:T(8,128)(2,1)S(1)}, bf16[1024,256]{1,0:T(8,128)(2,1)}, u32[]{:S(2)}) copy-start(bf16[1024,256]{1,0:T(8,128)(2,1)} %param.20) | copy-start | bytes 1572868
  37.6 5.8 %copy-start.21 = (f32[768]{0:T(1024)}, f32[768]{0:T(1024)S(1)}, u32[]{:S(2)}) copy-start(f32[768]{0:T(1024)S(1)} %multiply_reduce_fusion.5) | copy-start | bytes 9220
  37.7 13.0 %copy-start.13 = (bf16[1,96,256]{2,1,0:T(8,128)(2,1)S(1)}, bf16[1,96,256]{2,1,0:T(8,128)(2,1)}, u32[]{:S(2)}) copy-start(bf16[1,96,256]{2,1,0:T(8,128)(2,1)} %param.13) | copy-start | bytes 147460
  40.3 10.7 %copy-start.25 = (f32[768]{0:T(1024)}, f32[768]{0:T(1024)S(1)}, u32[]{:S(2)}) copy-start(f32[768]{0:T(1024)S(1)} %rsqrt_reduce_fusion) | copy-start | bytes 9220
  42.6 0.9 copy-start.20
  42.6 14.2 %copy-start.17 = (bf16[1,768,256]{2,1,0:T(8,128)(2,1)S(1)}, bf16[1,768,256]{2,1,0:T(8,128)(2,1)}, u32[]{:S(2)}) copy-start(bf16[1,768,256]{2,1,0:T(8,128)(2,1)} %param.14) | copy-start | bytes 1179652
  45.3 13.5 %copy-start.10 = (bf16[512,512]{1,0:T(8,128)(2,1)S(1)}, bf16[512,512]{1,0:T(8,128)(2,1)}, u32[]{:S(2)}) copy-start(bf16[512,512]{1,0:T(8,128)(2,1)} %all_gather.49) | copy-start | bytes 1572868
  54.5 30.1 %reduce-scatter.9.cloned.1.call-start = ((), (), s32[]{:S(2)}) async-start(), calls=%async_computation.10 | async-start | bytes 786432 | tf_op jit(solution)/shard_map/reduce_scatter | solution.py:199
  61.8 4.2 %copy-start.22 = (f32[768]{0:T(1024)S(1)}, f32[768]{0:T(1024)}, u32[]{:S(2)}) copy-start(f32[768]{0:T(1024)} %copy-done.21) | copy-start | bytes 9220
  61.8 4.2 %copy-start.24 = (s32[768]{0:T(1024)S(1)}, s32[768]{0:T(1024)}, u32[]{:S(2)}) copy-start(s32[768]{0:T(1024)} %param.16) | copy-start | bytes 9220
  61.8 4.2 %copy-start.26 = (f32[768]{0:T(1024)S(1)}, f32[768]{0:T(1024)}, u32[]{:S(2)}) copy-start(f32[768]{0:T(1024)} %copy-done.25) | copy-start | bytes 9220
  61.8 4.2 %copy-start.31 = (pred[768]{0:T(1024)(128)(4,1)S(1)}, pred[768]{0:T(1024)(128)(4,1)}, u32[]{:S(2)}) copy-start(pred[768]{0:T(1024)(128)(4,1)} %copy-done.30) | copy-start | bytes 2308
  63.9 35.0 %reduce-scatter.7.cloned.1.call-start = ((), (), s32[]{:S(2)}) async-start(), calls=%async_computation.9 | async-start | bytes 393216 | tf_op jit(solution)/shard_map/reduce_scatter | solution.py:196
  65.3 0.7 copy-start.14
  72.8 46.4 %reduce-scatter.5.cloned.1.call-start = ((), (), s32[]{:S(2)}) async-start(), calls=%async_computation.8 | async-start | bytes 1179648 | tf_op jit(solution)/shard_map/reduce_scatter | solution.py:193
  72.9 1.8 copy-start.5
  72.9 1.8 copy-start.7
  72.9 1.8 %copy-start.9 = (bf16[768,512]{0,1:T(8,128)(2,1)S(1)}, bf16[768,512]{0,1:T(8,128)(2,1)}, u32[]{:S(2)}) copy-start(bf16[768,512]{0,1:T(8,128)(2,1)} %copy-done.8) | copy-start | bytes 2359300
  74.7 1.8 copy-start.27
  76.4 92.4 %all-reduce.5.cloned.1.call-start = ((), (), s32[]{:S(2)}) async-start(), calls=%async_computation.12 | async-start | bytes 1835008 | tf_op jit(solution)/shard_map/psum | solution.py:207
  119.2 0.8 copy-start.29
  120.1 5.8 %copy-start.15 = (f32[96,512]{1,0:T(8,128)S(1)}, f32[96,512]{1,0:T(8,128)}, u32[]{:S(2)}) copy-start(f32[96,512]{1,0:T(8,128)} %copy-done.14) | copy-start | bytes 589828
  121.2 10.4 %all-to-all-start.1 = ((bf16[4,12,256]{2,1,0:T(8,128)(2,1)}), bf16[4,12,256]{2,1,0:T(8,128)(2,1)S(1)}, u32[]{:S(2)}, u32[]{:S(2)}) async-start(bf16[4,12,256]{2,1,0:T(8,128)(2,1)} %convert_element_type.110), calls=%async_computation.1 | async-start | bytes 65536 | tf_op jit(solution)/shard_map/all_to_all | solution.py:165
  168.8 3.8 %copy-start.19 = (bf16[256,256]{1,0:T(8,128)(2,1)S(1)}, bf16[256,256]{1,0:T(8,128)(2,1)}, u32[]{:S(2)}) copy-start(bf16[256,256]{1,0:T(8,128)(2,1)} %get-tuple-element.25) | copy-start | bytes 393220
  168.8 4.5 %copy-start.18 = (bf16[256,256]{1,0:T(8,128)(2,1)S(1)}, bf16[256,256]{1,0:T(8,128)(2,1)}, u32[]{:S(2)}) copy-start(bf16[256,256]{1,0:T(8,128)(2,1)} %get-tuple-element.27) | copy-start | bytes 393220
Sparse Core Ops, SparseCore 0:
  10.4 12.1 all-gather.4
  24.1 11.2 all-gather.6
  119.4 49.4 all-reduce.4
Sparse Core Ops, SparseCore 1:
  54.6 12.7 reduce-scatter.10
  70.1 14.4 reduce-scatter.8
  87.3 11.6 reduce-scatter.6
  101.8 17.3 reduce-scatter.4
where the time goes:
time: 182 us; the launch traced here: 181 us
  waiting for transfers between devices  81.4 us (45%)
  blocking collectives  41.1 us (23%)
  matrix products  16.7 us (9%)
  between operations  16 us (9%)
  starting transfers between devices  11.2 us (6%)
  other arithmetic  7.66 us (4%)
  local copies, waits for them, and re-layouts  7.38 us (4%)
    psum x1, waiting for transfers between devices, shards(): lax.psum(shares[0].astype(jnp.bfloat16), 'dom').astype(jnp.float32)  36.5 us
    reduce_scatter x1, waiting for transfers between devices, shards(): lax.psum_scatter(grad_edge_in.astype(jnp.bfloat16), 'dp', scatter_dimensi...  20.3 us
    reduce_scatter x1, waiting for transfers between devices, shards(): lax.psum_scatter(grad_edge_out.astype(jnp.bfloat16), 'dp', scatter_dimens...  14.3 us
    all_gather x6, blocking collectives, widen_one(): return lax.all_gather(pieces, 'feat', axis=1, tiled=True)  13.2 us
    psum x4, blocking collectives, feat_total(): return lax.psum(values, 'feat')  9.88 us
    dot_general x7, matrix products, product_tn(): lax.dot_general(first, second, (((0,), (0,)), ((), ())), preferred_elemen...  7.11 us
    all_to_all x1, starting transfers between devices, shards(): lax.all_to_all(outgoing, 'dom', split_axis=0, concat_axis=0, tiled=True)  6.32 us
    psum x2, blocking collectives, feat_pair(): return lax.psum((first, second), 'feat')  4.96 us
  transfers between devices with their start and end apart: 9, of which 5 were waited for; matrix products, arithmetic and copies ran while one was open for 14% of the time, Pallas kernels for 0%

commit v1 on v0

v1 whole, which is shorter than its diff:
```python
import functools
import math

import jax
import jax.numpy as jnp
from jax import lax
from jax.experimental import pallas as pl
from jax.experimental.pallas import tpu as pltpu
from jax.sharding import PartitionSpec as P

EPSILON = 1e-05
F32 = jnp.float32
BF16 = jnp.bfloat16
CHUNK = 128
SLOT = 16


def product(first, second):
    return jnp.dot(first, second, preferred_element_type=F32)


def product_tn(first, second):
    return lax.dot_general(first, second, (((0,), (0,)), ((), ())), preferred_element_type=F32)


def product_nt(first, second):
    return lax.dot_general(first, second, (((1,), (1,)), ((), ())), preferred_element_type=F32)


def silu_and_slope(v):
    s = 1.0 / (1.0 + jnp.exp(-v))
    return v * s, s * (1.0 + v * (1.0 - s))


def round_up(value, step):
    return -(-value // step) * step


def norm_forward(lo, hi, width):
    mean = (jnp.sum(lo, axis=1, keepdims=True) + jnp.sum(hi, axis=1, keepdims=True)) / width
    lo, hi = lo - mean, hi - mean
    spread = (
        jnp.sum(lo * lo, axis=1, keepdims=True) + jnp.sum(hi * hi, axis=1, keepdims=True)
    ) / width
    inv = lax.rsqrt(spread + EPSILON)
    return lo * inv, hi * inv, inv


def norm_backward(glo, ghi, nlo, nhi, inv, width):
    gm = (jnp.sum(glo, axis=1, keepdims=True) + jnp.sum(ghi, axis=1, keepdims=True)) / width
    cm = (
        jnp.sum(glo * nlo, axis=1, keepdims=True) + jnp.sum(ghi * nhi, axis=1, keepdims=True)
    ) / width
    return inv * (glo - gm - nlo * cm), inv * (ghi - gm - nhi * cm)


def kernel(
    cfg,
    nodes, edges, gnodes, gedges, w_ei, w_eo, w_ni, w_no, snd, rcv, halo,
    o_nodes, o_edges, res,
    table, gn, e, ge, wei, weo, wni, wno,
    hout, hot_s, hot_r, x, pre, act, normed, msg_part, msg_other,
    n_in, n_act, n_og, n_pg, sgrad, eog, epg, dbuf, np_send, np_recv, tg, hback,
    fsend, frecv, own, dw, xrecv, share, up, child,
    loc, fs, fr, hs, hr, ts, tr, xs, xr, us, ur, ds, dr,
):
    nD, nS, N, R, K = cfg["nD"], cfg["nS"], cfg["N"], cfg["R"], cfg["HALO"]
    H = 256
    D = 2 * H
    Tp = table.shape[1]
    HP = halo.shape[1]
    d, s, f = lax.axis_index("dom"), lax.axis_index("dp"), lax.axis_index("feat")
    g = 1 - f
    pending = []

    def remote(src, dst, ss, rs, dev):
        cp = pltpu.make_async_remote_copy(
            src_ref=src, dst_ref=dst, send_sem=ss, recv_sem=rs,
            device_id=dev, device_id_type=pl.DeviceIdType.MESH,
        )
        return cp

    def send(src, dst, ss, rs, dev):
        cp = remote(src, dst, ss, rs, dev)
        cp.start()
        pending.append(cp)

    partner = {"feat": g}

    mine = pl.ds(pl.multiple_of(f * R, R), R)
    theirs = pl.ds(pl.multiple_of(g * R, R), R)
    locals_ = [
        (nodes.at[0], table.at[f, pl.ds(0, N)]),
        (edges.at[0, mine], e.at[f]),
        (w_ei, wei.at[f]),
        (w_eo, weo.at[f]),
        (gnodes.at[0], gn.at[f]),
        (w_ni, wni.at[f]),
        (w_no, wno.at[f]),
        (gedges.at[0, mine], ge.at[f]),
    ]
    lcp = []
    for i, (a, b) in enumerate(locals_):
        c = pltpu.make_async_copy(a, b, loc.at[i])
        c.start()
        lcp.append(c)

    bar = pltpu.get_barrier_semaphore()

    def greet(dev):
        pl.semaphore_signal(bar, inc=1, device_id=dev, device_id_type=pl.DeviceIdType.MESH)

    greet(partner)
    for o in range(1, nD):
        q = lax.rem(d + o, nD)
        for h in range(2):
            greet({"dom": q, "feat": h})
    for o in range(1, nS):
        greet({"dp": lax.rem(s + o, nS)})

    for h in range(2):
        table[h, pl.ds(pl.multiple_of(N + d * SLOT, SLOT), SLOT), :] = jnp.zeros((SLOT, H), BF16)
        hback[h, pl.ds(pl.multiple_of(d * SLOT, SLOT), SLOT), :] = jnp.zeros((SLOT, H), BF16)
        if Tp > N + nD * SLOT:
            table[h, N + nD * SLOT :, :] = jnp.zeros((Tp - N - nD * SLOT, H), BF16)
        if HP > nD * SLOT:
            hback[h, nD * SLOT :, :] = jnp.zeros((HP - nD * SLOT, H), BF16)
    cols = pl.ds(pl.multiple_of(f * R, 128), R)
    t = snd[:, cols]
    far = jnp.maximum(t - N, 0)
    q_of = lax.shift_right_logical(far * cfg["MUL"], 19)
    t = jnp.where(t < N, t, t + q_of * (SLOT - K))
    hot_s[...] = jnp.where(
        lax.broadcasted_iota(jnp.int32, (Tp, R), 0) == t, 1.0, 0.0
    ).astype(BF16)
    hot_r[...] = jnp.where(
        lax.broadcasted_iota(jnp.int32, (N, R), 0) == rcv[:, cols], 1.0, 0.0
    ).astype(BF16)
    hot_h = jnp.where(
        lax.broadcasted_iota(jnp.int32, (N, HP), 0) == halo[...], 1.0, 0.0
    ).astype(BF16)
    lcp[0].wait()
    hout[...] = product_tn(hot_h, table[f, :N, :]).astype(BF16)

    pl.semaphore_wait(bar, 1 + 2 * (nD - 1) + (nS - 1))

    for o in range(1, nD):
        q = lax.rem(d + o, nD)
        for h in range(2):
            send(
                hout.at[pl.ds(pl.multiple_of(q * SLOT, SLOT), SLOT)],
                table.at[f, pl.ds(pl.multiple_of(N + d * SLOT, SLOT), SLOT)],
                hs.at[q, h], hr.at[d, f], {"dom": q, "feat": h},
            )
    rem_src = [
        nodes.at[0], edges.at[0, theirs], w_ei, w_eo, gnodes.at[0], w_ni, w_no,
        gedges.at[0, theirs],
    ]
    for i, src in enumerate(rem_src):
        send(src, locals_[i][1], fs.at[i], fr.at[i], partner)
    arrive = [
        table.at[g, pl.ds(0, N)], e.at[g], wei.at[g], weo.at[g], gn.at[g], wni.at[g], wno.at[g],
        ge.at[g],
    ]

    def got(i):
        if i:
            lcp[i].wait()
        remote(arrive[i], arrive[i], fs.at[i], fr.at[i], partner).wait_recv()

    got(0)
    got(1)
    for h in range(2):
        x[:, h * H : (h + 1) * H] = e[h]
        x[:, 2 * D + h * H : 2 * D + (h + 1) * H] = product_tn(
            hot_r[...], table[h, :N, :]
        ).astype(BF16)
    for o in range(1, nD):
        q = lax.rem(d + nD - o, nD)
        for h in range(2):
            dst = table.at[h, pl.ds(pl.multiple_of(N + q * SLOT, SLOT), SLOT)]
            remote(dst, dst, hs.at[q, h], hr.at[q, h], partner).wait_recv()
    for h in range(2):
        x[:, D + h * H : D + (h + 1) * H] = product_tn(hot_s[...], table[h]).astype(BF16)
    got(2)
    for h in range(2):
        v = product(x[...], wei[h])
        pre[h] = v
        a, _ = silu_and_slope(v)
        act[:, h * H : (h + 1) * H] = a.astype(BF16)
    got(3)
    lo, hi, inv = norm_forward(product(act[...], weo[0]), product(act[...], weo[1]), D)
    normed[0], normed[1] = lo, hi
    e_inv = inv
    msg_part[:, :H] = product(hot_r[...], lo.astype(BF16))
    msg_part[:, H:] = product(hot_r[...], hi.astype(BF16))
    send(msg_part, msg_other, fs.at[8], fr.at[8], partner)
    got(4)
    got(5)
    n_in[:, :H] = table[0, :N, :]
    n_in[:, H:D] = table[1, :N, :]
    first = [product(n_in[:, :D], wni[h, :D, :]) for h in range(2)]
    remote(msg_other, msg_other, fs.at[8], fr.at[8], partner).wait_recv()
    n_in[:, D:] = (msg_part[...] + msg_other[...]).astype(BF16)
    slopes = []
    for h in range(2):
        v = first[h] + product(n_in[:, D:], wni[h, D:, :])
        a, b = silu_and_slope(v)
        slopes.append(b)
        n_act[:, h * H : (h + 1) * H] = a.astype(BF16)
    got(6)
    lo, hi, inv = norm_forward(product(n_act[...], wno[0]), product(n_act[...], wno[1]), D)
    lo, hi = norm_backward(gn[0].astype(F32), gn[1].astype(F32), lo, hi, inv, D)
    n_og[0], n_og[1] = lo.astype(BF16), hi.astype(BF16)
    v = product_nt(n_og[0], wno[0]) + product_nt(n_og[1], wno[1])
    n_pg[0] = (v[:, :H] * slopes[0]).astype(BF16)
    n_pg[1] = (v[:, H:] * slopes[1]).astype(BF16)
    v = product_nt(n_pg[0], wni[0, D:, :]) + product_nt(n_pg[1], wni[1, D:, :])
    sgrad[...] = v.astype(BF16)

    sizes = [D // nS // CHUNK, 2 * D // nS // CHUNK, D // nS // CHUNK, 3 * D // nS // CHUNK]
    bases = [0, sizes[0], sizes[0] + sizes[1], sizes[0] + sizes[1] + sizes[2]]
    nch = sum(sizes)
    efirst = bases[2]

    def block(ref, i, sp):
        w = sizes[i] * CHUNK
        return ref[:, pl.ds(pl.multiple_of(sp * w, CHUNK), w)]

    def ship(i, sp):
        for j in range(sizes[i]):
            c = bases[i] + j
            send(dw.at[sp, c], xrecv.at[s, c], xs.at[sp, c], xr.at[s, c], {"dp": sp})

    for i, lhs, rhs in ((0, n_act, n_og), (1, n_in, n_pg)):
        for o in list(range(1, nS)) + [0]:
            sp = lax.rem(s + o, nS)
            v = product_tn(block(lhs, i, sp), rhs[f]) * cfg["node_factor"]
            dw[sp, bases[i] : bases[i] + sizes[i]] = v.reshape(sizes[i], CHUNK, H).astype(BF16)
            if o:
                ship(i, sp)

    root = nD // 2 - 1
    left = d < root
    side = jnp.where(left, 0, 1)
    is_root = d == root
    leaf = jnp.logical_or(d == 0, d == nD - 1)
    toward = jnp.where(left, d + 1, jnp.maximum(d - 1, 0))
    away = jnp.where(left, jnp.maximum(d - 1, 0), jnp.minimum(d + 1, nD - 1))

    def up_copy(c):
        return remote(up.at[c], child.at[side, c], us.at[c], ur.at[side, c], {"dom": toward})

    def child_wait(k, c):
        remote(up.at[c], child.at[k, c], us.at[c], ur.at[k, c], {"dom": toward}).wait_recv()

    def down_copy(c, k, dev):
        return remote(res.at[c], res.at[c], ds.at[k, c], dr.at[c], {"dom": dev})

    def stage_a(c):
        total = dw[s, c].astype(F32)
        for o in range(1, nS):
            sp = lax.rem(s + o, nS)
            remote(dw.at[sp, c], xrecv.at[sp, c], xs.at[sp, c], xr.at[sp, c], {"dp": sp}).wait_recv()
            total += xrecv[sp, c].astype(F32)

        @pl.when(leaf)
        def _():
            up[c] = total.astype(BF16)
            up_copy(c).start()

        @pl.when(jnp.logical_not(leaf))
        def _():
            share[c] = total

    def stage_b(c):
        @pl.when(jnp.logical_not(jnp.logical_or(leaf, is_root)))
        def _():
            child_wait(side, c)
            up[c] = (share[c] + child[side, c].astype(F32)).astype(BF16)
            up_copy(c).start()

    def stage_r(c):
        @pl.when(is_root)
        def _():
            child_wait(0, c)
            child_wait(1, c)
            res[c] = (share[c] + child[0, c].astype(F32) + child[1, c].astype(F32)).astype(BF16)
            down_copy(c, 0, root - 1).start()
            down_copy(c, 1, root + 1).start()

    def stage_d(c):
        @pl.when(jnp.logical_not(is_root))
        def _():
            down_copy(c, 0, away).wait_recv()

            @pl.when(jnp.logical_not(leaf))
            def _():
                down_copy(c, 0, away).start()

    def step(tt):
        for fn, lag in ((stage_a, 0), (stage_b, 1), (stage_r, 2), (stage_d, 4)):
            c = tt - lag
            if 0 <= c < nch:
                fn(c)

    clock = [0]

    def advance(limit):
        while clock[0] < limit:
            step(clock[0])
            clock[0] += 1

    got(7)
    live = product_tn(hot_r[...], jnp.ones((N, 128), BF16))[:, :1]
    glo = live * (ge[0].astype(F32) + product_tn(hot_r[...], sgrad[:, :H]))
    ghi = live * (ge[1].astype(F32) + product_tn(hot_r[...], sgrad[:, H:]))
    lo, hi = norm_backward(glo, ghi, normed[0], normed[1], e_inv, D)
    eog[0], eog[1] = lo.astype(BF16), hi.astype(BF16)
    v = product_nt(eog[0], weo[0]) + product_nt(eog[1], weo[1])
    for h in range(2):
        _, b = silu_and_slope(pre[h])
        epg[h] = (v[:, h * H : (h + 1) * H] * b).astype(BF16)

    order = list(range(1, nS)) + [0]
    edge_items = ((2, act, eog), (3, x, epg))
    for i, lhs, rhs in edge_items:
        lo_c = bases[i] - efirst
        for o in order:
            sp = lax.rem(s + o, nS)
            v = product_tn(block(lhs, i, sp), rhs[g]) * cfg["edge_factor"]
            fsend[sp, lo_c : lo_c + sizes[i]] = v.reshape(sizes[i], CHUNK, H).astype(BF16)
            part = pl.ds(lo_c, sizes[i])
            k = 11 + (i - 2) * nS
            send(fsend.at[sp, part], frecv.at[sp, part], fs.at[k + sp], fr.at[k + sp], partner)
    for i, lhs, rhs in edge_items:
        lo_c = bases[i] - efirst
        part = pl.ds(lo_c, sizes[i])
        k = 11 + (i - 2) * nS
        for o in order:
            sp = lax.rem(s + o, nS)
            v = product_tn(block(lhs, i, sp), rhs[f]) * cfg["edge_factor"]
            dst = frecv.at[sp, part]
            remote(dst, dst, fs.at[k + sp], fr.at[k + sp], partner).wait_recv()
            v = v.reshape(sizes[i], CHUNK, H) + frecv[sp, lo_c : lo_c + sizes[i]].astype(F32)
            dw[sp, bases[i] : bases[i] + sizes[i]] = v.astype(BF16)
            if o:
                ship(i, sp)
    advance(efirst)

    for hh in range(2):
        h = g if hh == 0 else f
        rows = pl.ds(pl.multiple_of(h * H, H), H)
        v = product_nt(epg[0], wei[0, rows, :]) + product_nt(epg[1], wei[1, rows, :])
        out = (ge[h].astype(F32) + v.astype(BF16).astype(F32)).astype(BF16)
        if hh == 0:
            dbuf[...] = out
            send(dbuf, o_edges.at[mine], fs.at[9], fr.at[9], partner)
        else:
            o_edges[mine, :] = out
    for hh in range(2):
        h = g if hh == 0 else f
        rows_s = pl.ds(pl.multiple_of(D + h * H, H), H)
        rows_r = pl.ds(pl.multiple_of(2 * D + h * H, H), H)
        vs = (product_nt(epg[0], wei[0, rows_s, :]) + product_nt(epg[1], wei[1, rows_s, :])).astype(BF16)
        vr = (product_nt(epg[0], wei[0, rows_r, :]) + product_nt(epg[1], wei[1, rows_r, :])).astype(BF16)
        tgv = product(hot_s[...], vs)
        tg[h] = tgv[N : N + nD * SLOT].astype(BF16)
        for o in range(1, nD):
            q = lax.rem(d + o, nD)
            send(
                tg.at[h, pl.ds(pl.multiple_of(q * SLOT, SLOT), SLOT)],
                hback.at[f, pl.ds(pl.multiple_of(d * SLOT, SLOT), SLOT)],
                ts.at[q, h], tr.at[d, f], {"dom": q, "feat": h},
            )
        nv = tgv[:N] + product(hot_r[...], vr)
        if hh == 0:
            np_send[...] = nv
            send(np_send, np_recv, fs.at[10], fr.at[10], partner)
    rows = pl.ds(pl.multiple_of(f * H, H), H)
    nv += product_nt(n_pg[0], wni[0, rows, :]) + product_nt(n_pg[1], wni[1, rows, :])
    remote(np_recv, np_recv, fs.at[10], fr.at[10], partner).wait_recv()
    nv += np_recv[...]
    for o in range(1, nD):
        q = lax.rem(d + nD - o, nD)
        for h in range(2):
            dst = hback.at[h, pl.ds(pl.multiple_of(q * SLOT, SLOT), SLOT)]
            remote(dst, dst, ts.at[q, h], tr.at[q, h], partner).wait_recv()
    hot_h = jnp.where(
        lax.broadcasted_iota(jnp.int32, (N, HP), 0) == halo[...], 1.0, 0.0
    ).astype(BF16)
    nv += product(hot_h, hback[0]) + product(hot_h, hback[1])
    o_nodes[...] = nv.astype(BF16)
    advance(nch + 5)
    dst = o_edges.at[theirs]
    remote(dst, dst, fs.at[9], fr.at[9], partner).wait_recv()

    for cp in pending:
        cp.wait_send()
    for c in range(nch):
        @pl.when(jnp.logical_not(is_root))
        def _():
            up_copy(c).wait_send()

        @pl.when(jnp.logical_or(is_root, jnp.logical_not(leaf)))
        def _():
            down_copy(c, 0, away).wait_send()

        @pl.when(is_root)
        def _():
            down_copy(c, 1, away).wait_send()


def shards(node_latents, edge_latents, grad_nodes, grad_edges, edge_sender, edge_receiver,
           halo_rows, w_ei, w_eo, w_ni, w_no):
    nD, nS = lax.axis_size("dom"), lax.axis_size("dp")
    N, EC = node_latents.shape[1], edge_latents.shape[1]
    H = node_latents.shape[2]
    D = 2 * H
    R = EC // 2
    K = halo_rows.shape[2]
    HP = round_up(nD * SLOT, 128)
    Tp = round_up(N + nD * SLOT, 128)
    mul = -(-(1 << 19) // K)
    assert all((v * mul) >> 19 == v // K for v in range(nD * K))
    halo = jnp.pad(halo_rows[0], ((0, 0), (0, SLOT - K)), constant_values=-1).reshape(1, -1)
    if HP > nD * SLOT:
        halo = jnp.pad(halo, ((0, 0), (0, HP - nD * SLOT)), constant_values=-1)
    nch = 7 * D // nS // CHUNK
    nce = 4 * D // nS // CHUNK
    cfg = dict(
        nD=nD, nS=nS, N=N, R=R, HALO=K, MUL=mul,
        edge_factor=1.0 / math.sqrt(nS * EC * nD), node_factor=1.0 / math.sqrt(nS * N * nD),
    )
    vm = lambda shape, dt=BF16: pltpu.VMEM(shape, dt)
    sem = lambda *shape: pltpu.SemaphoreType.DMA(shape)
    any_, vmem = pl.BlockSpec(memory_space=pl.ANY), pl.BlockSpec(memory_space=pltpu.VMEM)
    scratch = [
        vm((2, Tp, H)), vm((2, N, H)), vm((2, R, H)), vm((2, R, H)),
        vm((2, 3 * D, H)), vm((2, D, H)), vm((2, 2 * D, H)), vm((2, D, H)),
        vm((HP, H)), vm((Tp, R)), vm((N, R)), vm((R, 3 * D)), vm((2, R, H), F32), vm((R, D)),
        vm((2, R, H), F32), vm((N, D), F32), vm((N, D), F32),
        vm((N, 2 * D)), vm((N, D)), vm((2, N, H)), vm((2, N, H)), vm((N, D)),
        vm((2, R, H)), vm((2, R, H)), vm((R, H)), vm((N, H), F32), vm((N, H), F32),
        vm((2, nD * SLOT, H)), vm((2, HP, H)),
        vm((nS, nce, CHUNK, H)), vm((nS, nce, CHUNK, H)), vm((8, 128), F32),
        vm((nS, nch, CHUNK, H)), vm((nS, nch, CHUNK, H)), vm((nch, CHUNK, H), F32),
        vm((nch, CHUNK, H)), vm((2, nch, CHUNK, H)),
        sem(8), sem(11 + 2 * nS), sem(11 + 2 * nS), sem(nD, 2), sem(nD, 2), sem(nD, 2), sem(nD, 2),
        sem(nS, nch), sem(nS, nch), sem(nch), sem(2, nch), sem(2, nch), sem(nch),
    ]
    d_nodes, d_edges, dw = pl.pallas_call(
        functools.partial(kernel, cfg),
        out_shape=(
            jax.ShapeDtypeStruct((N, H), BF16),
            jax.ShapeDtypeStruct((EC, H), BF16),
            jax.ShapeDtypeStruct((nch, CHUNK, H), BF16),
        ),
        in_specs=[any_] * 8 + [vmem] * 3,
        out_specs=(vmem, vmem, vmem),
        scratch_shapes=scratch,
        compiler_params=pltpu.CompilerParams(
            collective_id=0, has_side_effects=True, vmem_limit_bytes=50 * 1024 * 1024
        ),
        cost_estimate=pl.CostEstimate(
            flops=4_000_000_000, bytes_accessed=8_000_000, transcendentals=1_000_000
        ),
    )(node_latents, edge_latents, grad_nodes, grad_edges, w_ei, w_eo, w_ni, w_no,
      edge_sender.reshape(1, -1), edge_receiver.reshape(1, -1), halo)
    dw = dw.reshape(nch * CHUNK, H)
    a, b = D // nS, 2 * D // nS
    g_no, g_ni = dw[:a], dw[a : a + b]
    g_eo, g_ei = dw[a + b : 2 * a + b], dw[2 * a + b :]
    return (d_nodes[None], d_edges[None], g_ei.astype(F32), g_eo.astype(F32), g_ni.astype(F32),
            g_no.astype(F32))


def solution(mesh):
    whole = P(("group", "dp"), "dom", "feat")
    weight = P(None, "feat")
    share = P(("group", "dp"), "feat")
    return jax.shard_map(
        shards,
        mesh=mesh,
        in_specs=(whole,) * 4 + (P("dom"), P("dom"), P("dom", None, None)) + (weight,) * 4,
        out_specs=(whole, whole, share, share, share, share),
        check_vma=False,
    )
```

time: 182 us -> 92.2 us (0.51)
  the two profiles are of different devices: /device:TPU:0 before, /device:TPU:24 now
where the time goes in v1:
time: 92.2 us; the launch traced here: 91.6 us
  Pallas kernels  77.8 us (84%)
  local copies, waits for them, and re-layouts  10.5 us (11%)
  other arithmetic  2.65 us (3%)
    pallas_call x1, Pallas kernels, shards(): pl.pallas_call(functools.partial(kernel, cfg), out_shape=(jax.ShapeDtypeS...  77.8 us
    unnamed x22, local copies, waits for them, and re-layouts  9.69 us

profile of v1, /device:TPU:24, one launch (start us, length us, event | category | flops | bytes accessed | tf_op | source)
XLA Modules:
  0.0 91.6 jit_solution(5693972211914291527)
XLA Ops:
  0.6 0.0 copy-start.8
  0.6 0.7 pad.8
  1.3 0.1 reshape.36
  1.4 0.0 copy-start.9
  1.4 0.0 copy-done.8
  1.4 0.7 copy-done.9
  2.1 0.0 copy-start
  2.1 1.1 %copy-done = bf16[1536,256]{1,0:T(8,128)(2,1)S(1)} copy-done((bf16[1536,256]{1,0:T(8,128)(2,1)S(1)}, bf16[1536,256]{1,0:T(8,128)(2,1)}, u32[]{:S(2)}) %copy-start) | copy-done | bytes 786456
  3.2 0.0 copy-start.1
  3.2 1.0 %copy-done.1 = bf16[1024,256]{1,0:T(8,128)(2,1)S(1)} copy-done((bf16[1024,256]{1,0:T(8,128)(2,1)S(1)}, bf16[1024,256]{1,0:T(8,128)(2,1)}, u32[]{:S(2)}) %copy-start.1) | copy-done | bytes 524312
  4.3 0.0 copy-start.2
  4.3 1.0 %copy-done.2 = bf16[1,768,256]{2,1,0:T(8,128)(2,1)S(1)} copy-done((bf16[1,768,256]{2,1,0:T(8,128)(2,1)S(1)}, bf16[1,768,256]{2,1,0:T(8,128)(2,1)}, u32[]{:S(2)}) %copy-start.2) | copy-done | bytes 393240
  5.3 0.0 copy-start.3
  5.3 1.0 %copy-done.3 = bf16[1,768,256]{2,1,0:T(8,128)(2,1)S(1)} copy-done((bf16[1,768,256]{2,1,0:T(8,128)(2,1)S(1)}, bf16[1,768,256]{2,1,0:T(8,128)(2,1)}, u32[]{:S(2)}) %copy-start.3) | copy-done | bytes 393240
  6.3 0.0 copy-start.4
  6.3 0.9 %copy-done.4 = bf16[512,256]{1,0:T(8,128)(2,1)S(1)} copy-done((bf16[512,256]{1,0:T(8,128)(2,1)S(1)}, bf16[512,256]{1,0:T(8,128)(2,1)}, u32[]{:S(2)}) %copy-start.4) | copy-done | bytes 262168
  7.2 0.0 copy-start.5
  7.2 0.9 %copy-done.5 = bf16[512,256]{1,0:T(8,128)(2,1)S(1)} copy-done((bf16[512,256]{1,0:T(8,128)(2,1)S(1)}, bf16[512,256]{1,0:T(8,128)(2,1)}, u32[]{:S(2)}) %copy-start.5) | copy-done | bytes 262168
  8.2 0.0 copy-start.6
  8.2 0.8 copy-done.6
  9.0 0.0 copy-start.7
  9.0 0.8 copy-done.7
  9.8 77.8 %shard_map.154 = (bf16[96,256]{1,0:T(8,128)(2,1)S(1)}, bf16[768,256]{1,0:T(8,128)(2,1)S(1)}, bf16[14,128,256]{2,1,0:T(8,128)(2,1)S(1)}) custom-call(bf16[1,96,256]{2,1,0:T(8,128)(2,1)S(1)} %copy-done.6, bf16[1,768,256]{2,1,0:T(8,128)(2,1)S(1)} %copy-done.2, bf16[1,96,256]{2,1,0:T(8,128)(2,1)S(1)} %copy-done.7, bf16[1,768,256]{2,1,0:T(8,128)(2,1)S(1)} %copy-done.3, ...), custom_call_target="tpu_custom_call" | custom-call | flops 4000000000 | bytes 8000000 | tf_op jit(solution)/shard_map/pallas_call | solution.py:452
  87.6 0.8 bitcast_convert_fusion.1
  88.5 0.8 bitcast_convert_fusion.2
  89.3 1.0 %bitcast_convert_fusion = f32[768,256]{1,0:T(8,128)} fusion(bf16[6,128,256]{2,1,0:T(8,128)(2,1)S(1)} %slice.16), kind=kLoop, calls=%fused_computation | loop fusion | flops 196608 | bytes 1179648 | tf_op jit(solution)/shard_map/convert_element_type | solution.py:474
  90.3 0.6 copy.19
  90.9 0.7 copy.20
  (6 shorter events, 0.1 us)
Async XLA Ops:
  0.6 0.8 copy-start.8
  1.4 0.7 copy-start.9
  2.1 1.1 %copy-start = (bf16[1536,256]{1,0:T(8,128)(2,1)S(1)}, bf16[1536,256]{1,0:T(8,128)(2,1)}, u32[]{:S(2)}) copy-start(bf16[1536,256]{1,0:T(8,128)(2,1)} %w_ei.1) | copy-start | bytes 2359300
  3.2 1.0 %copy-start.1 = (bf16[1024,256]{1,0:T(8,128)(2,1)S(1)}, bf16[1024,256]{1,0:T(8,128)(2,1)}, u32[]{:S(2)}) copy-start(bf16[1024,256]{1,0:T(8,128)(2,1)} %w_ni.1) | copy-start | bytes 1572868
  4.3 1.0 %copy-start.2 = (bf16[1,768,256]{2,1,0:T(8,128)(2,1)S(1)}, bf16[1,768,256]{2,1,0:T(8,128)(2,1)}, u32[]{:S(2)}) copy-start(bf16[1,768,256]{2,1,0:T(8,128)(2,1)} %edges.1) | copy-start | bytes 1179652
  5.3 1.0 %copy-start.3 = (bf16[1,768,256]{2,1,0:T(8,128)(2,1)S(1)}, bf16[1,768,256]{2,1,0:T(8,128)(2,1)}, u32[]{:S(2)}) copy-start(bf16[1,768,256]{2,1,0:T(8,128)(2,1)} %gedges.1) | copy-start | bytes 1179652
  6.3 0.9 %copy-start.4 = (bf16[512,256]{1,0:T(8,128)(2,1)S(1)}, bf16[512,256]{1,0:T(8,128)(2,1)}, u32[]{:S(2)}) copy-start(bf16[512,256]{1,0:T(8,128)(2,1)} %w_eo.1) | copy-start | bytes 786436
  7.2 0.9 %copy-start.5 = (bf16[512,256]{1,0:T(8,128)(2,1)S(1)}, bf16[512,256]{1,0:T(8,128)(2,1)}, u32[]{:S(2)}) copy-start(bf16[512,256]{1,0:T(8,128)(2,1)} %w_no.1) | copy-start | bytes 786436
  8.2 0.8 copy-start.6
  9.0 0.8 copy-start.7

commit v2 on v1

--- a/solution.py
+++ b/solution.py
@@ -13,6 +13,7 @@
 BF16 = jnp.bfloat16
 CHUNK = 128
 SLOT = 16
+LAG_B, LAG_R, LAG_D = 3, 6, 10
 
 
 def product(first, second):
@@ -56,7 +57,7 @@
 
 def kernel(
     cfg,
-    nodes, edges, gnodes, gedges, w_ei, w_eo, w_ni, w_no, snd, rcv, halo,
+    nodes, edges, gnodes, gedges, w_ei, w_eo, w_ni, w_no, ints,
     o_nodes, o_edges, res,
     table, gn, e, ge, wei, weo, wni, wno,
     hout, hot_s, hot_r, x, pre, act, normed, msg_part, msg_other,
@@ -68,7 +69,7 @@
     H = 256
     D = 2 * H
     Tp = table.shape[1]
-    HP = halo.shape[1]
+    HP = hout.shape[0]
     d, s, f = lax.axis_index("dom"), lax.axis_index("dp"), lax.axis_index("feat")
     g = 1 - f
     pending = []
@@ -126,7 +127,7 @@
         if HP > nD * SLOT:
             hback[h, nD * SLOT :, :] = jnp.zeros((HP - nD * SLOT, H), BF16)
     cols = pl.ds(pl.multiple_of(f * R, 128), R)
-    t = snd[:, cols]
+    t = ints[:, cols]
     far = jnp.maximum(t - N, 0)
     q_of = lax.shift_right_logical(far * cfg["MUL"], 19)
     t = jnp.where(t < N, t, t + q_of * (SLOT - K))
@@ -134,10 +135,10 @@
         lax.broadcasted_iota(jnp.int32, (Tp, R), 0) == t, 1.0, 0.0
     ).astype(BF16)
     hot_r[...] = jnp.where(
-        lax.broadcasted_iota(jnp.int32, (N, R), 0) == rcv[:, cols], 1.0, 0.0
+        lax.broadcasted_iota(jnp.int32, (N, R), 0) == ints[:, pl.ds(pl.multiple_of(2 * R + f * R, 128), R)], 1.0, 0.0
     ).astype(BF16)
     hot_h = jnp.where(
-        lax.broadcasted_iota(jnp.int32, (N, HP), 0) == halo[...], 1.0, 0.0
+        lax.broadcasted_iota(jnp.int32, (N, HP), 0) == ints[:, 4 * R :], 1.0, 0.0
     ).astype(BF16)
     lcp[0].wait()
     hout[...] = product_tn(hot_h, table[f, :N, :]).astype(BF16)
@@ -299,7 +300,7 @@
                 down_copy(c, 0, away).start()
 
     def step(tt):
-        for fn, lag in ((stage_a, 0), (stage_b, 1), (stage_r, 2), (stage_d, 4)):
+        for fn, lag in ((stage_a, 0), (stage_b, LAG_B), (stage_r, LAG_R), (stage_d, LAG_D)):
             c = tt - lag
             if 0 <= c < nch:
                 fn(c)
@@ -317,23 +318,19 @@
     ghi = live * (ge[1].astype(F32) + product_tn(hot_r[...], sgrad[:, H:]))
     lo, hi = norm_backward(glo, ghi, normed[0], normed[1], e_inv, D)
     eog[0], eog[1] = lo.astype(BF16), hi.astype(BF16)
-    v = product_nt(eog[0], weo[0]) + product_nt(eog[1], weo[1])
-    for h in range(2):
-        _, b = silu_and_slope(pre[h])
-        epg[h] = (v[:, h * H : (h + 1) * H] * b).astype(BF16)
-
     order = list(range(1, nS)) + [0]
-    edge_items = ((2, act, eog), (3, x, epg))
-    for i, lhs, rhs in edge_items:
+
+    def across(i, lhs, rhs):
         lo_c = bases[i] - efirst
+        part = pl.ds(lo_c, sizes[i])
+        k = 11 + (i - 2) * nS
         for o in order:
             sp = lax.rem(s + o, nS)
             v = product_tn(block(lhs, i, sp), rhs[g]) * cfg["edge_factor"]
             fsend[sp, lo_c : lo_c + sizes[i]] = v.reshape(sizes[i], CHUNK, H).astype(BF16)
-            part = pl.ds(lo_c, sizes[i])
-            k = 11 + (i - 2) * nS
             send(fsend.at[sp, part], frecv.at[sp, part], fs.at[k + sp], fr.at[k + sp], partner)
-    for i, lhs, rhs in edge_items:
+
+    def combine(i, lhs, rhs):
         lo_c = bases[i] - efirst
         part = pl.ds(lo_c, sizes[i])
         k = 11 + (i - 2) * nS
@@ -346,7 +343,18 @@
             dw[sp, bases[i] : bases[i] + sizes[i]] = v.astype(BF16)
             if o:
                 ship(i, sp)
-    advance(efirst)
+
+    across(2, act, eog)
+    v = product_nt(eog[0], weo[0]) + product_nt(eog[1], weo[1])
+    for h in range(2):
+        _, b = silu_and_slope(pre[h])
+        epg[h] = (v[:, h * H : (h + 1) * H] * b).astype(BF16)
+    combine(2, act, eog)
+    advance(3)
+    across(3, x, epg)
+    advance(6)
+    combine(3, x, epg)
+    advance(efirst + 2)
 
     for hh in range(2):
         h = g if hh == 0 else f
@@ -358,6 +366,7 @@
             send(dbuf, o_edges.at[mine], fs.at[9], fr.at[9], partner)
         else:
             o_edges[mine, :] = out
+    advance(efirst + 4)
     for hh in range(2):
         h = g if hh == 0 else f
         rows_s = pl.ds(pl.multiple_of(D + h * H, H), H)
@@ -374,6 +383,7 @@
                 ts.at[q, h], tr.at[d, f], {"dom": q, "feat": h},
             )
         nv = tgv[:N] + product(hot_r[...], vr)
+        advance(efirst + 6 + 2 * hh)
         if hh == 0:
             np_send[...] = nv
             send(np_send, np_recv, fs.at[10], fr.at[10], partner)
@@ -387,11 +397,11 @@
             dst = hback.at[h, pl.ds(pl.multiple_of(q * SLOT, SLOT), SLOT)]
             remote(dst, dst, ts.at[q, h], tr.at[q, h], partner).wait_recv()
     hot_h = jnp.where(
-        lax.broadcasted_iota(jnp.int32, (N, HP), 0) == halo[...], 1.0, 0.0
+        lax.broadcasted_iota(jnp.int32, (N, HP), 0) == ints[:, 4 * R :], 1.0, 0.0
     ).astype(BF16)
     nv += product(hot_h, hback[0]) + product(hot_h, hback[1])
     o_nodes[...] = nv.astype(BF16)
-    advance(nch + 5)
+    advance(nch + LAG_D)
     dst = o_edges.at[theirs]
     remote(dst, dst, fs.at[9], fr.at[9], partner).wait_recv()
 
@@ -409,6 +419,15 @@
         @pl.when(is_root)
         def _():
             down_copy(c, 1, away).wait_send()
+
+
+def spread(rows, nodes, edges, dw, o_nodes, o_edges, *outs):
+    o_nodes[0] = nodes[...]
+    o_edges[0] = edges[...]
+    at = 0
+    for r, out in zip(rows, outs):
+        out[...] = dw[at : at + r].astype(F32).reshape(r * CHUNK, dw.shape[2])
+        at += r
 
 
 def shards(node_latents, edge_latents, grad_nodes, grad_edges, edge_sender, edge_receiver,
@@ -423,9 +442,10 @@
     Tp = round_up(N + nD * SLOT, 128)
     mul = -(-(1 << 19) // K)
     assert all((v * mul) >> 19 == v // K for v in range(nD * K))
-    halo = jnp.pad(halo_rows[0], ((0, 0), (0, SLOT - K)), constant_values=-1).reshape(1, -1)
-    if HP > nD * SLOT:
-        halo = jnp.pad(halo, ((0, 0), (0, HP - nD * SLOT)), constant_values=-1)
+    halo = jnp.pad(
+        halo_rows[0], ((0, HP // SLOT - nD), (0, SLOT - K)), constant_values=-1
+    ).reshape(-1)
+    ints = jnp.concatenate([edge_sender, edge_receiver, halo]).reshape(1, -1)
     nch = 7 * D // nS // CHUNK
     nce = 4 * D // nS // CHUNK
     cfg = dict(
@@ -456,23 +476,31 @@
             jax.ShapeDtypeStruct((EC, H), BF16),
             jax.ShapeDtypeStruct((nch, CHUNK, H), BF16),
         ),
-        in_specs=[any_] * 8 + [vmem] * 3,
+        in_specs=[any_] * 8 + [vmem],
         out_specs=(vmem, vmem, vmem),
         scratch_shapes=scratch,
         compiler_params=pltpu.CompilerParams(
-            collective_id=0, has_side_effects=True, vmem_limit_bytes=50 * 1024 * 1024
+            collective_id=0, has_side_effects=True, vmem_limit_bytes=62 * 1024 * 1024
         ),
         cost_estimate=pl.CostEstimate(
             flops=4_000_000_000, bytes_accessed=8_000_000, transcendentals=1_000_000
         ),
     )(node_latents, edge_latents, grad_nodes, grad_edges, w_ei, w_eo, w_ni, w_no,
-      edge_sender.reshape(1, -1), edge_receiver.reshape(1, -1), halo)
-    dw = dw.reshape(nch * CHUNK, H)
-    a, b = D // nS, 2 * D // nS
-    g_no, g_ni = dw[:a], dw[a : a + b]
-    g_eo, g_ei = dw[a + b : 2 * a + b], dw[2 * a + b :]
-    return (d_nodes[None], d_edges[None], g_ei.astype(F32), g_eo.astype(F32), g_ni.astype(F32),
-            g_no.astype(F32))
+      ints)
+    rows = (D // nS // CHUNK, 2 * D // nS // CHUNK, D // nS // CHUNK, 3 * D // nS // CHUNK)
+    out = lambda r: jax.ShapeDtypeStruct((r * CHUNK, H), F32)
+    d_nodes, d_edges, g_no, g_ni, g_eo, g_ei = pl.pallas_call(
+        functools.partial(spread, rows),
+        out_shape=(
+            jax.ShapeDtypeStruct((1, N, H), BF16), jax.ShapeDtypeStruct((1, EC, H), BF16),
+            out(rows[0]), out(rows[1]), out(rows[2]), out(rows[3]),
+        ),
+        in_specs=[vmem] * 3,
+        out_specs=(vmem,) * 6,
+        compiler_params=pltpu.CompilerParams(vmem_limit_bytes=62 * 1024 * 1024),
+        cost_estimate=pl.CostEstimate(flops=500_000, bytes_accessed=4_000_000, transcendentals=0),
+    )(d_nodes, d_edges, dw)
+    return d_nodes, d_edges, g_ei, g_eo, g_ni, g_no
 
 
 def solution(mesh):

time: 92.2 us -> 60 us (0.65)
  Pallas kernels: 77.8 us -> 57.7 us
  local copies, waits for them, and re-layouts: 10.5 us -> 1.39 us
  other arithmetic: 2.65 us -> 0.01 us
    pallas_call x1, Pallas kernels: 77.8 us -> 55 us  [shards(): pl.pallas_call(functools.partial(kernel, cfg), out_shape=(jax.ShapeDtypeS...]
    unnamed x22 -> x4, local copies, waits for them, and re-layouts: 9.69 us -> 0.01 us
    pallas_call x0 -> x1, Pallas kernels: none -> 2.73 us  [shards(): pl.pallas_call(functools.partial(spread, rows), out_shape=(jax.ShapeDtype...]
    convert_element_type x3 -> x0, other arithmetic: 2.65 us -> none  [the longest x1 0.96 us: shards(): g_ei.astype(F32)]
where the time goes in v2:
time: 60 us; the launch traced here: 59.8 us
  Pallas kernels  57.7 us (96%)
  local copies, waits for them, and re-layouts  1.39 us (2%)
  between operations  0.67 us (1%)
    pallas_call x1, Pallas kernels, shards(): pl.pallas_call(functools.partial(kernel, cfg), out_shape=(jax.ShapeDtypeS...  55 us
    pallas_call x1, Pallas kernels, shards(): pl.pallas_call(functools.partial(spread, rows), out_shape=(jax.ShapeDtype...  2.73 us

profile of v2, /device:TPU:24, one launch (start us, length us, event | category | flops | bytes accessed | tf_op | source)
XLA Modules:
  0.0 59.8 jit_solution(7623319200539262914)
XLA Ops:
  0.6 0.0 copy-start
  0.6 0.0 copy-start.1
  0.7 0.7 %pad.4 = s32[8,16]{1,0:T(8,128)S(1)} pad(s32[4,12]{1,0:T(4,128)} %bitcast.1, s32[]{:T(128)} %constant.0.clone.1), padding=0_4x0_4 | pad | bytes 708 | tf_op jit(solution)/shard_map/jit(_pad)/pad | solution.py:445
  1.4 0.1 reshape.18
  1.4 0.0 copy-done
  1.4 0.0 copy-done.1
  1.5 0.6 %reshape.19.ints = s32[1,1664]{1,0:T(1,128)} reshape(s32[1664]{0:T(1024)S(1)} %pad_add_fusion) | data formatting | bytes 13312 | tf_op jit(solution)/shard_map/reshape | solution.py:448
  2.1 55.0 %shard_map.154 = (bf16[96,256]{1,0:T(8,128)(2,1)}, bf16[768,256]{1,0:T(8,128)(2,1)}, bf16[14,128,256]{2,1,0:T(8,128)(2,1)}) custom-call(bf16[1,96,256]{2,1,0:T(8,128)(2,1)} %nodes.1, bf16[1,768,256]{2,1,0:T(8,128)(2,1)} %edges.1, bf16[1,96,256]{2,1,0:T(8,128)(2,1)} %gnodes.1, bf16[1,768,256]{2,1,0:T(8,128)(2,1)} %gedges.1, bf16[1536,256]{1,0:T(8,128)(2,1)} %w_ei.1, ...), custom_call_target="tpu_custom_call" | custom-call | flops 4000000000 | bytes 8000000 | tf_op jit(solution)/shard_map/pallas_call | solution.py:472
  57.0 2.7 %shard_map.155 = (bf16[1,96,256]{2,1,0:T(8,128)(2,1)}, bf16[1,768,256]{2,1,0:T(8,128)(2,1)}, f32[256,256]{1,0:T(8,128)}, f32[512,256]{1,0:T(8,128)}, f32[256,256]{1,0:T(8,128)}, /*index=5*/f32[768,256]{1,0:T(8,128)}) custom-call(bf16[96,256]{1,0:T(8,128)(2,1)} %get-tuple-element.15.nodes, bf16[768,256]{1,0:T(8,128)(2,1)} %get-tuple-element.16.edges, ...), custom_call_target="tpu_custom_call" | custom-call | flops 500000 | bytes 4000000 | tf_op jit(solution)/shard_map/pallas_call | solution.py:492
  (1 shorter events, 0.0 us)
Async XLA Ops:
  0.6 0.8 %copy-start = (s32[768]{0:T(1024)S(1)}, s32[768]{0:T(1024)}, u32[]{:S(2)}) copy-start(s32[768]{0:T(1024)} %param.16) | copy-start | bytes 9220
  0.6 0.8 %copy-start.1 = (s32[768]{0:T(1024)S(1)}, s32[768]{0:T(1024)}, u32[]{:S(2)}) copy-start(s32[768]{0:T(1024)} %param.15) | copy-start | bytes 9220

commit v3 on v2

--- a/solution.py
+++ b/solution.py
@@ -13,7 +13,7 @@
 BF16 = jnp.bfloat16
 CHUNK = 128
 SLOT = 16
-LAG_B, LAG_R, LAG_D = 3, 6, 10
+LAG_B, LAG_R, LAG_D = 3, 6, 9
 
 
 def product(first, second):

time: 60 us -> 59.6 us (level)
  no operation moved by 1% of the time
where the time goes in v3:
time: 59.6 us; the launch traced here: 59.4 us
  Pallas kernels  57.3 us (96%)
  local copies, waits for them, and re-layouts  1.39 us (2%)
  between operations  0.67 us (1%)
    pallas_call x1, Pallas kernels, shards(): pl.pallas_call(functools.partial(kernel, cfg), out_shape=(jax.ShapeDtypeS...  54.6 us
    pallas_call x1, Pallas kernels, shards(): pl.pallas_call(functools.partial(spread, rows), out_shape=(jax.ShapeDtype...  2.73 us

profile of v3, /device:TPU:24, one launch (start us, length us, event | category | flops | bytes accessed | tf_op | source)
XLA Modules:
  0.0 59.4 jit_solution(6150817630348119086)
XLA Ops:
  0.6 0.0 copy-start
  0.6 0.0 copy-start.1
  0.7 0.7 %pad.4 = s32[8,16]{1,0:T(8,128)S(1)} pad(s32[4,12]{1,0:T(4,128)} %bitcast.1, s32[]{:T(128)} %constant.0.clone.1), padding=0_4x0_4 | pad | bytes 708 | tf_op jit(solution)/shard_map/jit(_pad)/pad | solution.py:445
  1.4 0.1 reshape.18
  1.4 0.0 copy-done
  1.4 0.0 copy-done.1
  1.5 0.6 %reshape.19.ints = s32[1,1664]{1,0:T(1,128)} reshape(s32[1664]{0:T(1024)S(1)} %pad_add_fusion) | data formatting | bytes 13312 | tf_op jit(solution)/shard_map/reshape | solution.py:448
  2.1 54.6 %shard_map.154 = (bf16[96,256]{1,0:T(8,128)(2,1)}, bf16[768,256]{1,0:T(8,128)(2,1)}, bf16[14,128,256]{2,1,0:T(8,128)(2,1)}) custom-call(bf16[1,96,256]{2,1,0:T(8,128)(2,1)} %nodes.1, bf16[1,768,256]{2,1,0:T(8,128)(2,1)} %edges.1, bf16[1,96,256]{2,1,0:T(8,128)(2,1)} %gnodes.1, bf16[1,768,256]{2,1,0:T(8,128)(2,1)} %gedges.1, bf16[1536,256]{1,0:T(8,128)(2,1)} %w_ei.1, ...), custom_call_target="tpu_custom_call" | custom-call | flops 4000000000 | bytes 8000000 | tf_op jit(solution)/shard_map/pallas_call | solution.py:472
  56.7 2.7 %shard_map.155 = (bf16[1,96,256]{2,1,0:T(8,128)(2,1)}, bf16[1,768,256]{2,1,0:T(8,128)(2,1)}, f32[256,256]{1,0:T(8,128)}, f32[512,256]{1,0:T(8,128)}, f32[256,256]{1,0:T(8,128)}, /*index=5*/f32[768,256]{1,0:T(8,128)}) custom-call(bf16[96,256]{1,0:T(8,128)(2,1)} %get-tuple-element.15.nodes, bf16[768,256]{1,0:T(8,128)(2,1)} %get-tuple-element.16.edges, ...), custom_call_target="tpu_custom_call" | custom-call | flops 500000 | bytes 4000000 | tf_op jit(solution)/shard_map/pallas_call | solution.py:492
  (1 shorter events, 0.0 us)
Async XLA Ops:
  0.6 0.8 %copy-start = (s32[768]{0:T(1024)S(1)}, s32[768]{0:T(1024)}, u32[]{:S(2)}) copy-start(s32[768]{0:T(1024)} %param.16) | copy-start | bytes 9220
  0.6 0.8 %copy-start.1 = (s32[768]{0:T(1024)S(1)}, s32[768]{0:T(1024)}, u32[]{:S(2)}) copy-start(s32[768]{0:T(1024)} %param.15) | copy-start | bytes 9220
